TPU v7x, 256 devices: a whole 4x4x8 slice. The times are simulated.
256 devices in a mesh: dp: 8 (over y, core), fsdp: 32 (over x, z).
Axes of the slice: x: 4, y: 4, z: 8, core: 2. Of those that a mesh axis runs over, the one named last changes fastest.
Arguments:
- grad_parts: bfloat16 [8, 256, 512, 512], P('dp', None, 'fsdp'), may hold values from -6 to 6
- first_moment: bfloat16 [256, 512, 512], P('dp', 'fsdp'), may hold values from -4 to 4
- second_moment: float32 [256, 512, 512], P('dp', 'fsdp'), may hold values from 0.25 to 4
- left_basis: bfloat16 [8, 32, 2, 512, 512], P('dp', 'fsdp'), may hold values from -0.25 to 0.25
- right_basis: bfloat16 [8, 32, 2, 512, 512], P('dp', 'fsdp'), may hold values from -0.25 to 0.25
- owner_list: int32 [8, 32, 1], P('dp'), may hold values from 0 to 31; in each aligned block of 32 rows (0 to 31, 32 to 63, ..., all dimensions but the last counted through in order) at most 2 rows name the same one
Outputs:
- first_moment_new: bfloat16 [256, 512, 512], P('dp', 'fsdp')
- second_moment_new: float32 [256, 512, 512], P('dp', 'fsdp')
- update: bfloat16 [256, 512, 512], P('dp', 'fsdp')
Inputs may be any that keep to these rules, and one draw needn't show every extreme that they name: `owner_list`: in each data group no owner holds more than 2 blocks, and some owner holds exactly 2.
All inputs are finite; a program needn't handle non-finite values.
Results may differ from a plain program's by a relative error of at most 0.022.
Values may be sent and summed in bfloat16 or wider, within the bound.
A program may use at most 64 MiB of HBM per device.

v0:
```python
import jax
import jax.numpy as jnp
from jax import lax
from jax.sharding import PartitionSpec as P

BETA_FIRST = 0.9
BETA_SECOND = 0.95
EPSILON = 1e-08


def slot_numbers(owners):
    how_many = owners.shape[0]
    ordinal = jnp.arange(how_many, dtype=jnp.int32)
    matching = owners[:, None] == owners[None, :]
    earlier = ordinal[None, :] < ordinal[:, None]
    return jnp.sum(jnp.logical_and(matching, earlier).astype(jnp.int32), axis=1)


def adam_rotated(rotated, moment_one, moment_two):
    rotated_wide = rotated.astype(jnp.float32)
    first_wide = BETA_FIRST * moment_one.astype(jnp.float32) + (1.0 - BETA_FIRST) * rotated_wide
    second_new = BETA_SECOND * moment_two + (1.0 - BETA_SECOND) * rotated_wide * rotated_wide
    direction = (first_wide / (jnp.sqrt(second_new) + EPSILON)).astype(jnp.bfloat16)
    return (first_wide.astype(jnp.bfloat16), second_new, direction)


def rotate_forward(gathered, left_side, right_side):
    half_rot = jnp.einsum(
        "sij,sjk->sik", gathered, right_side, preferred_element_type=jnp.float32
    ).astype(jnp.bfloat16)
    return jnp.einsum(
        "sji,sjk->sik", left_side, half_rot, preferred_element_type=jnp.float32
    ).astype(jnp.bfloat16)


def rotate_backward(direction, left_side, right_side):
    back_half = jnp.einsum(
        "sij,skj->sik", direction, right_side, preferred_element_type=jnp.float32
    ).astype(jnp.bfloat16)
    return jnp.einsum(
        "sij,sjk->sik", left_side, back_half, preferred_element_type=jnp.float32
    ).astype(jnp.bfloat16)


def to_slots(held_rows, source, filled, owners_count, capacity):
    padded = jnp.concatenate([held_rows, jnp.zeros_like(held_rows[:1])], axis=0)
    chosen = jnp.where(filled, source, held_rows.shape[0])
    return padded[chosen].reshape((owners_count, capacity) + held_rows.shape[1:])


def from_slots(received, target):
    flattened = received.reshape((-1,) + received.shape[2:])
    return flattened[target]


def per_device(grad_parts, first_moment, second_moment, left_basis, right_basis, owner_list):
    owners_count = lax.axis_size("fsdp")
    capacity = left_basis.shape[2]
    partial_sum = grad_parts[0].astype(jnp.float32)
    gradient = lax.psum_scatter(
        partial_sum.astype(jnp.bfloat16), "dp", scatter_dimension=0, tiled=True
    )
    owners = owner_list[0, :, 0]
    blocks = owners.shape[0]
    target = owners * capacity + slot_numbers(owners)
    positions = jnp.arange(owners_count * capacity, dtype=jnp.int32)
    picked = positions[:, None] == target[None, :]
    source = jnp.sum(jnp.where(picked, jnp.arange(blocks, dtype=jnp.int32)[None, :], 0), axis=1)
    filled = jnp.any(picked, axis=1)
    left_side = left_basis[0, 0]
    right_side = right_basis[0, 0]
    outgoing = to_slots(gradient, source, filled, owners_count, capacity)
    gathered = lax.all_to_all(outgoing, "fsdp", split_axis=0, concat_axis=2, tiled=True)[0]
    rotated = rotate_forward(gathered, left_side, right_side)
    returned = lax.all_to_all(rotated[None], "fsdp", split_axis=2, concat_axis=0, tiled=True)
    rotated_rows = from_slots(returned, target)
    first_new, second_new, direction = adam_rotated(rotated_rows, first_moment, second_moment)
    direction_slots = to_slots(direction, source, filled, owners_count, capacity)
    direction_whole = lax.all_to_all(
        direction_slots, "fsdp", split_axis=0, concat_axis=2, tiled=True
    )[0]
    update_whole = rotate_backward(direction_whole, left_side, right_side)
    update_back = lax.all_to_all(
        update_whole[None], "fsdp", split_axis=2, concat_axis=0, tiled=True
    )
    update_rows = from_slots(update_back, target)
    return (first_new, second_new, update_rows)


def solution(mesh):
    placed = (
        P("dp", None, "fsdp", None),
        P("dp", "fsdp", None),
        P("dp", "fsdp", None),
        P("dp", "fsdp", None, None, None),
        P("dp", "fsdp", None, None, None),
        P("dp", None, None),
    )
    return jax.shard_map(
        per_device,
        mesh=mesh,
        in_specs=placed,
        out_specs=(P("dp", "fsdp", None), P("dp", "fsdp", None), P("dp", "fsdp", None)),
        check_vma=False,
    )
```

profile of v0, /device:TPU:8, one launch (start us, length us, event | category | flops | bytes accessed | tf_op | source)
XLA Modules:
  0.0 211.6 jit_solution(13349624052458809443)
XLA Ops:
  7.2 0.0 copy-start
  7.2 0.0 reduce-scatter.2.cloned.1.call-start
  7.2 0.0 copy-start.2
  7.2 0.7 reduce-scatter.2.cloned.1.call-update
  7.9 0.0 copy-done.2
  8.0 0.2 convert_reduce_fusion
  8.1 0.1 select_reduce_fusion
  8.2 0.1 fusion.13
  8.4 41.9 %reduce-scatter.2.cloned.1.call-done = bf16[32,16,512]{2,1,0:T(8,128)(2,1)} async-done(((bf16[256,16,512]{2,1,0:T(8,128)(2,1)}), bf16[32,16,512]{2,1,0:T(8,128)(2,1)}) %reduce-scatter.2.cloned.1.call-update) | async-done | bytes 524304 | tf_op jit(solution)/shard_map/reduce_scatter | solution.py:60
  50.3 1.1 concatenate.6
  51.4 0.6 gather_fusion
  52.0 38.5 %all_to_all.60 = bf16[32,2,16,512]{3,2,1,0:T(8,128)(2,1)S(1)} all-to-all(bf16[32,2,16,512]{3,2,1,0:T(8,128)(2,1)S(1)} %bitcast.59), channel_id=1, replica_groups=mesh['dp'=8,'fsdp'=32] {'fsdp'}, dimensions={0} | all-to-all | bytes 2097152 | tf_op jit(solution)/shard_map/all_to_all | solution.py:73
  90.5 0.1 copy.32
  90.6 0.0 copy-done
  90.6 2.5 %fusion = bf16[1,2,512,512]{2,3,1,0:T(8,128)(2,1)S(1)} fusion(bf16[1,1,2,512,512]{4,3,2,1,0:T(8,128)(2,1)S(1)} %copy-done, bf16[2,512,512]{2,1,0:T(8,128)(2,1)S(1)} %bitcast.66, bf16[1,1,2,512,512]{4,3,2,1,0:T(8,128)(2,1)} %param.10), kind=kOutput, calls=%fused_computation.9 | convolution fusion | flops 1074790400 | bytes 4194304 | tf_op jit(solution)/shard_map/sji,sjk->sik/dot_general | solution.py:31
  93.1 2.1 copy.34
  95.2 5.1 %all-to-all-start.1 = ((bf16[1,2,512,512]{3,1,0,2:T(2,128)(2,1)}), bf16[1,2,512,512]{3,1,0,2:T(2,128)(2,1)S(1)}, u32[]{:S(2)}, u32[]{:S(2)}) async-start(bf16[1,2,512,512]{3,1,0,2:T(2,128)(2,1)} %copy.34), calls=%async_computation.2 | async-start | bytes 2097152 | tf_op jit(solution)/shard_map/all_to_all | solution.py:75
  100.3 28.2 %all-to-all-done.1 = bf16[1,2,512,512]{3,1,0,2:T(2,128)(2,1)S(1)} async-done(((bf16[1,2,512,512]{3,1,0,2:T(2,128)(2,1)}), bf16[1,2,512,512]{3,1,0,2:T(2,128)(2,1)S(1)}, u32[]{:S(2)}, u32[]{:S(2)}) %all-to-all-start.1) | async-done | bytes 1048608 | tf_op jit(solution)/shard_map/all_to_all | solution.py:75
  128.6 0.2 copy.35
  128.7 0.0 copy-start.1
  128.8 0.1 copy.36
  128.8 0.6 gather_fusion.1
  129.4 0.3 copy-done.1
  129.8 3.0 %divide_convert_fusion = (bf16[32,16,512]{2,1,0:T(8,128)(2,1)S(1)}, f32[32,16,512]{2,1,0:T(8,128)}, bf16[32,16,512]{2,1,0:T(8,128)(2,1)}) fusion(bf16[32,16,512]{2,1,0:T(8,128)(2,1)S(1)} %gather_fusion.1, bf16[32,16,512]{2,1,0:T(8,128)(2,1)S(1)} %copy-done.1, f32[32,16,512]{2,1,0:T(8,128)} %param.8), kind=kLoop, calls=%fused_computation.18 | loop fusion | flops 3407872 | bytes 4194304 | tf_op jit(solution)/shard_map/convert_element_type | solution.py:23
  132.9 0.6 gather_fusion.2
  133.5 33.0 %all_to_all.61 = bf16[32,2,16,512]{3,2,1,0:T(8,128)(2,1)S(1)} all-to-all(bf16[32,2,16,512]{3,2,1,0:T(8,128)(2,1)S(1)} %bitcast.58), channel_id=1, replica_groups=mesh['dp'=8,'fsdp'=32] {'fsdp'}, dimensions={0} | all-to-all | bytes 2097152 | tf_op jit(solution)/shard_map/all_to_all | solution.py:79
  166.5 0.1 copy.37
  166.6 2.5 %fusion.1 = bf16[1,2,512,512]{2,3,1,0:T(8,128)(2,1)S(1)} fusion(bf16[1,1,2,512,512]{4,3,2,1,0:T(8,128)(2,1)S(1)} %copy-done, bf16[2,512,512]{2,1,0:T(8,128)(2,1)S(1)} %bitcast.67, bf16[1,1,2,512,512]{4,3,2,1,0:T(8,128)(2,1)} %param.10), kind=kOutput, calls=%fused_computation.10 | convolution fusion | flops 1074790400 | bytes 4194304 | tf_op jit(solution)/shard_map/sij,sjk->sik/dot_general | solution.py:40
  169.1 1.0 copy.39
  170.1 33.0 %all_to_all.62 = bf16[1,2,512,512]{3,1,0,2:T(2,128)(2,1)S(1)} all-to-all(bf16[1,2,512,512]{3,1,0,2:T(2,128)(2,1)S(1)} %copy.39), channel_id=1, replica_groups=mesh['dp'=8,'fsdp'=32] {'fsdp'}, dimensions={2} | all-to-all | bytes 2097152 | tf_op jit(solution)/shard_map/all_to_all | solution.py:83
  203.1 0.2 copy.40
  203.3 0.1 copy.41
  203.4 1.4 gather_fusion.3
  (6 shorter events, 0.1 us)
Async XLA Ops:
  7.2 83.4 %copy-start = (bf16[1,1,2,512,512]{4,3,2,1,0:T(8,128)(2,1)S(1)}, bf16[1,1,2,512,512]{4,3,2,1,0:T(8,128)(2,1)}, u32[]{:S(2)}) copy-start(bf16[1,1,2,512,512]{4,3,2,1,0:T(8,128)(2,1)} %param.9) | copy-start | bytes 3145732
  7.2 43.1 %reduce-scatter.2.cloned.1.call-start = ((), (), s32[]{:S(2)}) async-start(), calls=%async_computation.5 | async-start | bytes 4718592 | tf_op jit(solution)/shard_map/reduce_scatter | solution.py:60
  7.2 0.7 copy-start.2
  95.2 33.4 %all-to-all-start.1 = ((bf16[1,2,512,512]{3,1,0,2:T(2,128)(2,1)}), bf16[1,2,512,512]{3,1,0,2:T(2,128)(2,1)S(1)}, u32[]{:S(2)}, u32[]{:S(2)}) async-start(bf16[1,2,512,512]{3,1,0,2:T(2,128)(2,1)} %copy.34), calls=%async_computation.2 | async-start | bytes 2097152 | tf_op jit(solution)/shard_map/all_to_all | solution.py:75
  128.7 1.0 copy-start.1
Sparse Core Ops, SparseCore 0:
  10.6 39.6 reduce-scatter.1
where the time goes:
time: 213 us; the launch traced here: 212 us
  blocking collectives  105 us (49%)
  waiting for transfers between devices  70.8 us (33%)
  between operations  14.2 us (7%)
  local copies, waits for them, and re-layouts  8.44 us (4%)
  starting transfers between devices  5.15 us (2%)
  matrix products  5 us (2%)
  other arithmetic  3.45 us (2%)
    reduce_scatter x1, waiting for transfers between devices, per_device(): lax.psum_scatter(partial_sum.astype(jnp.bfloat16), 'dp', scatter_dimensio...  41.9 us
    all_to_all x1, blocking collectives, per_device(): lax.all_to_all(outgoing, 'fsdp', split_axis=0, concat_axis=2, tiled=True)[0]  38.5 us
    all_to_all x1, blocking collectives, per_device(): lax.all_to_all(update_whole[None], 'fsdp', split_axis=2, concat_axis=0, t...  33 us
    all_to_all x1, blocking collectives, per_device(): lax.all_to_all(direction_slots, 'fsdp', split_axis=0, concat_axis=2, tile...  33 us
    all_to_all x1, waiting for transfers between devices, per_device(): lax.all_to_all(rotated[None], 'fsdp', split_axis=2, concat_axis=0, tiled=...  28.2 us
    all_to_all x1, starting transfers between devices, per_device(): lax.all_to_all(rotated[None], 'fsdp', split_axis=2, concat_axis=0, tiled=...  5.11 us
  transfers between devices with their start and end apart: 2, of which 2 were waited for; matrix products, arithmetic and copies ran while one was open for 0% of the time, Pallas kernels for 0%

commit v1 on v0

v1 whole, which is shorter than its diff:
```python
import functools

import jax
import jax.numpy as jnp
from jax import lax
from jax.experimental import pallas as pl
from jax.experimental.pallas import tpu as pltpu
from jax.sharding import PartitionSpec as P

BETA_FIRST = 0.9
BETA_SECOND = 0.95
EPSILON = 1e-08

MESH = pl.DeviceIdType.MESH
NY = 4
CUTS = 2
SLOTS = 2


def z_order(nz):
    order = [0]
    for step in range(1, nz // 2 + 1):
        order.append(step)
        if nz - step != step:
            order.append(nz - step)
    return order


def adam(rotated, first, second):
    wide = rotated.astype(jnp.float32)
    first_wide = BETA_FIRST * first.astype(jnp.float32) + (1.0 - BETA_FIRST) * wide
    second_new = BETA_SECOND * second + (1.0 - BETA_SECOND) * wide * wide
    return first_wide, second_new


def kernel(
    nx, nz,
    src, tgt, grads, first_hbm, second_hbm, left_hbm, right_hbm,
    first_out, second_out, update_out,
    own, other, far_up, far_down, from_down, from_up, grad,
    g_send, g_recv, r_send, r_recv, d_send, d_recv, u_send, u_recv,
    first, second, left, right, left_t, total, half, back, first_new, second_new, update,
    load_sem, own_sem, pair_send, pair_recv, y_send, y_recv,
    g_ssem, g_rsem, r_ssem, r_rsem, d_ssem, d_rsem, u_ssem, u_rsem, out_sem,
):
    nf = nx * nz
    nb, rows, columns = first.shape
    width = columns // CUTS
    d, me = lax.axis_index("dp"), lax.axis_index("fsdp")
    y, core = d // 2, d % 2
    x, z = me // nz, me % nz
    up, down = (y + 1) % NY, (y + NY - 1) % NY
    at_up, at_down, at_pair = (up * 2 + core, me), (down * 2 + core, me), (y * 2 + 1 - core, me)
    order = z_order(nz)

    chips = [(y + 2) % NY, up, down, y]
    loads = [
        pltpu.make_async_copy(ref, to, load_sem.at[i])
        for i, (ref, to) in enumerate(
            [(left_hbm, left), (right_hbm, right), (first_hbm, first), (second_hbm, second)]
        )
    ]
    cols = [pl.ds(c * width, width) for c in range(CUTS)]
    owns = [
        [
            pltpu.make_async_copy(grads.at[chips[r], core, :, :, cols[c]], own.at[c, r], own_sem.at[c, r])
            for r in range(NY)
        ]
        for c in range(CUTS)
    ]
    for c in range(CUTS):
        for r in range(NY):
            owns[c][r].start()
    for load in loads:
        load.start()

    barrier = pltpu.get_barrier_semaphore()

    def greet(i, carry):
        for dz in order:
            p = ((x + i) % nx) * nz + (z + dz) % nz
            if dz == 0:
                @pl.when(i > 0)
                def _():
                    pl.semaphore_signal(barrier, inc=1, device_id=(d, p), device_id_type=MESH)
            else:
                pl.semaphore_signal(barrier, inc=1, device_id=(d, p), device_id_type=MESH)
        return carry

    for device in (at_pair, at_up, at_down):
        pl.semaphore_signal(barrier, inc=1, device_id=device, device_id_type=MESH)
    lax.fori_loop(0, nx, greet, 0)
    pl.semaphore_wait(barrier, nf - 1 + 3)

    def remote(source, target, send, recv, device):
        return pltpu.make_async_remote_copy(
            src_ref=source, dst_ref=target, send_sem=send, recv_sem=recv, device_id=device, device_id_type=MESH
        )

    pairs = [
        [
            remote(
                grads.at[chips[r], 1 - core, :, :, cols[c]], other.at[c, r],
                pair_send.at[c, r], pair_recv.at[c, r], at_pair,
            )
            for r in range(NY)
        ]
        for c in range(CUTS)
    ]
    for c in range(CUTS):
        for r in range(NY):
            pairs[c][r].start()

    low, high = pl.ds(0, nb // 2), pl.ds(nb // 2, nb // 2)
    hops = [
        [
            remote(own.at[c, 0, low], far_up.at[c], y_send.at[c, 0], y_recv.at[c, 0], at_up),
            remote(own.at[c, 0, high], far_down.at[c], y_send.at[c, 1], y_recv.at[c, 1], at_down),
            remote(own.at[c, 1, high], from_down.at[c, high], y_send.at[c, 2], y_recv.at[c, 2], at_up),
            remote(own.at[c, 2, low], from_up.at[c, low], y_send.at[c, 3], y_recv.at[c, 3], at_down),
            remote(own.at[c, 1, low], from_down.at[c, low], y_send.at[c, 4], y_recv.at[c, 4], at_up),
            remote(own.at[c, 2, high], from_up.at[c, high], y_send.at[c, 5], y_recv.at[c, 5], at_down),
        ]
        for c in range(CUTS)
    ]
    group = min(4, nb // 2)

    def wide(ref, *at):
        return ref[at].astype(jnp.float32)

    def pair_sum(c, r):
        owns[c][r].wait()
        pairs[c][r].wait_recv()

        def step(j, carry):
            blocks = pl.ds(j * group, group)
            own[c, r, blocks] = (wide(own, c, r, blocks) + wide(other, c, r, blocks)).astype(jnp.bfloat16)
            return carry

        lax.fori_loop(0, nb // group, step, 0)

    def add_far(c, r, far, first_block):
        def step(j, carry):
            blocks = pl.ds(first_block + j * group, group)
            own[c, r, blocks] = (wide(own, c, r, blocks) + wide(far, c, pl.ds(j * group, group))).astype(jnp.bfloat16)
            return carry

        lax.fori_loop(0, nb // 2 // group, step, 0)

    def spread(c):
        pair_sum(c, 0)
        hops[c][0].start()
        hops[c][1].start()
        pair_sum(c, 1)
        hops[c][2].start()
        pair_sum(c, 2)
        hops[c][3].start()

    def forward(c):
        hops[c][0].wait_recv()
        add_far(c, 1, far_up, 0)
        hops[c][4].start()
        hops[c][1].wait_recv()
        add_far(c, 2, far_down, nb // 2)
        hops[c][5].start()

    def finish(c):
        pair_sum(c, 3)
        for i in (2, 3, 4, 5):
            hops[c][i].wait_recv()

        def step(j, carry):
            blocks = pl.ds(j * group, group)
            grad[c, blocks] = (
                wide(own, c, 3, blocks) + wide(from_down, c, blocks) + wide(from_up, c, blocks)
            ).astype(jnp.bfloat16)
            return carry

        lax.fori_loop(0, nb // group, step, 0)

    def exchange(send, recv, at, ssem, rsem, fill_plane=None, fill=None):
        def plane(i, carry):
            px = (x + i) % nx
            if fill_plane is not None:
                fill_plane(px)
            for dz in order:
                p = px * nz + (z + dz) % nz
                if fill is not None:
                    fill(p)
                source, target = send.at[(*at, p)], recv.at[(*at, me)]
                if dz == 0:
                    @pl.when(i > 0)
                    def _():
                        remote(source, target, ssem, rsem, (d, p)).start()

                    @pl.when(i == 0)
                    def _():
                        recv[(*at, me)] = send[(*at, me)]
                else:
                    remote(source, target, ssem, rsem, (d, p)).start()
            return carry

        lax.fori_loop(0, nx, plane, 0)

    def arrived(ref, at, rsem):
        whole = ref.at[(*at, pl.ds(0, nf - 1))]
        pltpu.make_async_copy(whole, whole, rsem).wait()

    def send_grad(c, s):
        def fill(p):
            g_send[c, s, p] = grad_cut[c][src[s * nf + p]]

        exchange(g_send, g_recv, (c, s), g_ssem.at[c, s], g_rsem.at[c, s], fill=fill)

    grad_cut = [grad.at[c] for c in range(CUTS)]

    spread(0)
    forward(0)
    spread(1)
    for load in loads:
        load.wait()
    for s in range(SLOTS):
        for t in range(nx):
            piece = pl.ds(t * nz * rows, nz * rows)
            left_t[s, :, piece] = left[s, piece, :].T
    finish(0)
    for s in range(SLOTS):
        send_grad(0, s)
    forward(1)
    finish(1)
    for s in range(SLOTS):
        send_grad(1, s)

    span = nz * rows

    def product(c, s, t):
        held = g_recv[c, s, pl.ds(t * nz, nz)].reshape(span, width)
        return jnp.dot(held, right[s, cols[c], :], preferred_element_type=jnp.float32)

    for s in range(SLOTS):
        arrived(g_recv, (0, s), g_rsem.at[0, s])

        def first_half(t, carry, s=s):
            total[s, pl.ds(t * span, span)] = product(0, s, t)
            return carry

        lax.fori_loop(0, nx, first_half, 0)

    for s in range(SLOTS):
        arrived(g_recv, (1, s), g_rsem.at[1, s])

        def second_half(t, carry, s=s):
            piece = pl.ds(t * span, span)
            half[s, piece] = (total[s, piece] + product(1, s, t)).astype(jnp.bfloat16)
            return carry

        lax.fori_loop(0, nx, second_half, 0)

        def rotate(px, s=s):
            made = jnp.dot(left_t[s, pl.ds(px * span, span)], half[s], preferred_element_type=jnp.float32)
            r_send[s, pl.ds(px * nz, nz)] = made.astype(jnp.bfloat16).reshape(nz, rows, columns)

        exchange(r_send, r_recv, (s,), r_ssem.at[s], r_rsem.at[s], fill_plane=rotate)

    for s in range(SLOTS):
        arrived(r_recv, (s,), r_rsem.at[s])

        def direct(p, s=s):
            block = src[s * nf + p]
            first_wide, second_wide = adam(r_recv[s, p], first[block], second[block])
            d_send[s, p] = (first_wide / (jnp.sqrt(second_wide) + EPSILON)).astype(jnp.bfloat16)

        exchange(d_send, d_recv, (s,), d_ssem.at[s], d_rsem.at[s], fill=direct)

    def moments(j, carry):
        first_wide, second_wide = adam(r_recv[tgt[j] // nf, tgt[j] % nf], first[j], second[j])
        first_new[j] = first_wide.astype(jnp.bfloat16)
        second_new[j] = second_wide
        return carry

    lax.fori_loop(0, nb, moments, 0)
    outs = [
        pltpu.make_async_copy(ref, to, out_sem.at[i])
        for i, (ref, to) in enumerate([(first_new, first_out), (second_new, second_out), (update, update_out)])
    ]
    outs[0].start()
    outs[1].start()

    for s in range(SLOTS):
        arrived(d_recv, (s,), d_rsem.at[s])

        def undo_right(t, carry, s=s):
            held = d_recv[s, pl.ds(t * nz, nz)].reshape(span, columns)
            made = lax.dot_general(held, right[s], (((1,), (1,)), ((), ())), preferred_element_type=jnp.float32)
            back[s, pl.ds(t * span, span)] = made.astype(jnp.bfloat16)
            return carry

        lax.fori_loop(0, nx, undo_right, 0)

        def undo_left(px, s=s):
            made = jnp.dot(left[s, pl.ds(px * span, span)], back[s], preferred_element_type=jnp.float32)
            u_send[s, pl.ds(px * nz, nz)] = made.astype(jnp.bfloat16).reshape(nz, rows, columns)

        exchange(u_send, u_recv, (s,), u_ssem.at[s], u_rsem.at[s], fill_plane=undo_left)

    for s in range(SLOTS):
        arrived(u_recv, (s,), u_rsem.at[s])

    def pick(j, carry):
        update[j] = u_recv[tgt[j] // nf, tgt[j] % nf]
        return carry

    lax.fori_loop(0, nb, pick, 0)
    outs[2].start()

    for c in range(CUTS):
        for r in range(NY):
            pairs[c][r].wait_send()
        for hop in hops[c]:
            hop.wait_send()
        for s in range(SLOTS):
            arrived(g_send, (c, s), g_ssem.at[c, s])
    for s in range(SLOTS):
        arrived(r_send, (s,), r_ssem.at[s])
        arrived(d_send, (s,), d_ssem.at[s])
        arrived(u_send, (s,), u_ssem.at[s])
    for out in outs:
        out.wait()


def tables(owners, nf):
    nb = owners.shape[0]
    ordinal = jnp.arange(nb, dtype=jnp.int32)
    matching = owners[:, None] == owners[None, :]
    earlier = ordinal[None, :] < ordinal[:, None]
    slot = jnp.sum(jnp.logical_and(matching, earlier).astype(jnp.int32), axis=1)
    target = slot * nf + owners
    picked = jnp.arange(SLOTS * nf, dtype=jnp.int32)[:, None] == target[None, :]
    source = jnp.sum(jnp.where(picked, ordinal[None, :], 0), axis=1)
    return source, target


def per_device(nx, nz, grad_parts, first_moment, second_moment, left_basis, right_basis, owner_list):
    nf = nx * nz
    nb, rows, columns = first_moment.shape
    width = columns // CUTS
    source, target = tables(owner_list[0, :, 0], nf)
    grads = grad_parts.reshape(NY, 2, nb, rows, columns)
    bf16, f32 = jnp.bfloat16, jnp.float32
    dma = pltpu.SemaphoreType.DMA
    order = nf * rows
    moved = pltpu.VMEM((SLOTS, nf, rows, columns), bf16)
    cut = pltpu.VMEM((CUTS, SLOTS, nf, rows, width), bf16)
    square = pltpu.VMEM((SLOTS, order, columns), bf16)
    hbm = pl.BlockSpec(memory_space=pl.ANY)
    smem = pl.BlockSpec(memory_space=pltpu.SMEM)
    return pl.pallas_call(
        functools.partial(kernel, nx, nz),
        out_shape=(
            jax.ShapeDtypeStruct((nb, rows, columns), bf16),
            jax.ShapeDtypeStruct((nb, rows, columns), f32),
            jax.ShapeDtypeStruct((nb, rows, columns), bf16),
        ),
        in_specs=[smem, smem, hbm, hbm, hbm, hbm, hbm],
        out_specs=(hbm, hbm, hbm),
        scratch_shapes=[
            pltpu.VMEM((CUTS, NY, nb, rows, width), bf16),
            pltpu.VMEM((CUTS, NY, nb, rows, width), bf16),
            pltpu.VMEM((CUTS, nb // 2, rows, width), bf16),
            pltpu.VMEM((CUTS, nb // 2, rows, width), bf16),
            pltpu.VMEM((CUTS, nb, rows, width), bf16),
            pltpu.VMEM((CUTS, nb, rows, width), bf16),
            pltpu.VMEM((CUTS, nb, rows, width), bf16),
            cut, cut, moved, moved, moved, moved, moved, moved,
            pltpu.VMEM((nb, rows, columns), bf16),
            pltpu.VMEM((nb, rows, columns), f32),
            square, square, square,
            pltpu.VMEM((SLOTS, order, columns), f32),
            square, square,
            pltpu.VMEM((nb, rows, columns), bf16),
            pltpu.VMEM((nb, rows, columns), f32),
            pltpu.VMEM((nb, rows, columns), bf16),
            dma((4,)), dma((CUTS, NY)), dma((CUTS, NY)), dma((CUTS, NY)), dma((CUTS, 6)), dma((CUTS, 6)),
            dma((CUTS, SLOTS)), dma((CUTS, SLOTS)),
            dma((SLOTS,)), dma((SLOTS,)), dma((SLOTS,)), dma((SLOTS,)), dma((SLOTS,)), dma((SLOTS,)),
            dma((3,)),
        ],
        compiler_params=pltpu.CompilerParams(
            collective_id=0, has_side_effects=True, vmem_limit_bytes=48 * 1024 * 1024
        ),
        cost_estimate=pl.CostEstimate(
            flops=SLOTS * 8 * order * columns * columns, bytes_accessed=16 * 1024 * 1024, transcendentals=0
        ),
    )(source, target, grads, first_moment, second_moment, left_basis[0, 0], right_basis[0, 0])


def solution(mesh):
    nf = mesh.shape["fsdp"]
    nz = min(8, nf // 2)
    placed = (
        P("dp", None, "fsdp", None),
        P("dp", "fsdp", None),
        P("dp", "fsdp", None),
        P("dp", "fsdp", None, None, None),
        P("dp", "fsdp", None, None, None),
        P("dp", None, None),
    )
    return jax.shard_map(
        functools.partial(per_device, nf // nz, nz),
        mesh=mesh,
        in_specs=placed,
        out_specs=(P("dp", "fsdp", None), P("dp", "fsdp", None), P("dp", "fsdp", None)),
        check_vma=False,
    )
```

time: 213 us -> 129 us (0.61)
  Pallas kernels: 0 us -> 117 us
  blocking collectives: 105 us -> 0 us
  waiting for transfers between devices: 70.8 us -> 0 us
  between operations: 14.2 us -> 0.65 us
  starting transfers between devices: 5.15 us -> 0 us
  matrix products: 5 us -> 0 us
    pallas_call x0 -> x1, Pallas kernels: none -> 117 us  [per_device(): pl.pallas_call(functools.partial(kernel, nx, nz), out_shape=(jax.ShapeDty...]
    all_to_all x3 -> x0, blocking collectives: 105 us -> none  [the longest x1 38.5 us: per_device(): lax.all_to_all(outgoing, 'fsdp', split_axis=0, concat_axis=2, tiled=True)[0]]
    reduce_scatter x1 -> x0, waiting for transfers between devices: 41.9 us -> none  [per_device(): lax.psum_scatter(partial_sum.astype(jnp.bfloat16), 'dp', scatter_dimensio...]
    all_to_all x1 -> x0, waiting for transfers between devices: 28.2 us -> none  [per_device(): lax.all_to_all(rotated[None], 'fsdp', split_axis=2, concat_axis=0, tiled=...]
    unnamed x6 -> x11, local copies, waits for them, and re-layouts: 0.41 us -> 7.27 us
    all_to_all x1 -> x0, starting transfers between devices: 5.11 us -> none  [per_device(): lax.all_to_all(rotated[None], 'fsdp', split_axis=2, concat_axis=0, tiled=...]
    dot_general x2 -> x0, matrix products: 5 us -> none  [the longest x1 2.51 us: rotate_backward(): jnp.einsum('sij,sjk->sik', left_side, back_half, preferred_element_type=j...]
    gather x4 -> x0, local copies, waits for them, and re-layouts: 3.18 us -> none  [the longest x2 1.95 us: from_slots(): return flattened[target]]
  transfers between devices with their start and end apart: 2 -> 0, of which waited for: 2 -> 0; matrix products, arithmetic and copies ran while one was open for 0% -> 0% of each run, Pallas kernels for 0% -> 0%
where the time goes in v1:
time: 129 us; the launch traced here: 127 us
  Pallas kernels  117 us (91%)
  local copies, waits for them, and re-layouts  7.27 us (6%)
  other arithmetic  1.67 us (1%)
    pallas_call x1, Pallas kernels, per_device(): pl.pallas_call(functools.partial(kernel, nx, nz), out_shape=(jax.ShapeDty...  117 us
    unnamed x11, local copies, waits for them, and re-layouts  7.27 us

profile of v1, /device:TPU:8, one launch (start us, length us, event | category | flops | bytes accessed | tf_op | source)
XLA Modules:
  0.0 126.9 jit_solution(2468792361071058651)
XLA Ops:
  0.6 0.9 convert_reduce_fusion
  1.5 0.7 multiply_add_fusion.tgt
  2.2 0.1 select_reduce_fusion.src
  2.3 0.0 copy-start
  2.3 1.2 copy-done
  3.5 0.0 copy-start.1
  3.5 1.2 copy-done.1
  4.7 0.0 copy-start.2
  4.7 1.2 copy-done.2
  6.0 0.0 copy-start.3
  6.0 1.0 copy-done.3
  7.0 117.3 %shard_map.85 = (bf16[32,16,512]{2,1,0:T(8,128)(2,1)S(1)}, f32[32,16,512]{2,1,0:T(8,128)S(1)}, bf16[32,16,512]{2,1,0:T(8,128)(2,1)S(1)}) custom-call(s32[64]{0:T(128)S(1)} %select_reduce_fusion.src, s32[32]{0:T(128)S(1)} %multiply_add_fusion.tgt, bf16[4,2,32,16,512]{4,3,2,1,0:T(8,128)(2,1)} %bitcast.7, bf16[32,16,512]{2,1,0:T(8,128)(2,1)S(1)} %copy-done.3, ...), custom_call_target="tpu_custom_call" | custom-call | flops 2147483648 | bytes 16777216 | tf_op jit(solution)/shard_map/pallas_call | solution.py:357
  124.3 0.8 copy.12
  125.1 1.0 copy.13
  126.1 0.8 copy.14
Async XLA Ops:
  2.3 1.2 copy-start
  3.5 1.2 copy-start.1
  4.7 1.2 copy-start.2
  6.0 1.0 copy-start.3

commit v2 on v1

v2 whole, which is shorter than its diff:
```python
import functools

import jax
import jax.numpy as jnp
from jax import lax
from jax.experimental import pallas as pl
from jax.experimental.pallas import tpu as pltpu
from jax.sharding import PartitionSpec as P

BETA_FIRST = 0.9
BETA_SECOND = 0.95
EPSILON = 1e-08

MESH = pl.DeviceIdType.MESH
VMEM_BYTES = 60 * 1024 * 1024
NY = 4
SLOTS = 2
CUTS = ((2, True, True), (2, False, True), (4, False, False))
NC = len(CUTS)


def column_cuts(columns):
    widths = [columns * eighths // 8 for eighths, _, _ in CUTS]
    return [sum(widths[:c]) for c in range(NC)], widths


def z_order(nz):
    order = [0]
    for step in range(1, nz // 2 + 1):
        order.append(step)
        if nz - step != step:
            order.append(nz - step)
    return order


def adam(rotated, first, second):
    wide = rotated.astype(jnp.float32)
    first_wide = BETA_FIRST * first.astype(jnp.float32) + (1.0 - BETA_FIRST) * wide
    second_new = BETA_SECOND * second + (1.0 - BETA_SECOND) * wide * wide
    return first_wide, second_new


def kernel(
    nx, nz,
    owners, grads, first_hbm, second_hbm, left_hbm, right_hbm,
    first_out, second_out, update_out,
    *scratch,
):
    cut_refs = [scratch[c * 8:c * 8 + 8] for c in range(NC)]
    own, other, far, from_down, from_up, grad, g_send, g_recv = zip(*cut_refs)
    (
        table, places,
        r_send, r_recv, d_send, d_recv, u_send, u_recv,
        first, second, left, right, left_t, total, half, back, first_new, second_new, update,
        load_sem, own_sem, pair_send, pair_recv, y_send, y_recv,
        g_ssem, g_rsem, r_ssem, r_rsem, d_ssem, d_rsem, u_ssem, u_rsem, out_sem,
    ) = scratch[NC * 8:]
    nf = nx * nz
    nb, rows, columns = first.shape
    starts, widths = column_cuts(columns)
    d, me = lax.axis_index("dp"), lax.axis_index("fsdp")
    y, core = d // 2, d % 2
    x, z = me // nz, me % nz
    up, down = (y + 1) % NY, (y + NY - 1) % NY
    at_up, at_down, at_pair = (up * 2 + core, me), (down * 2 + core, me), (y * 2 + 1 - core, me)
    at_far = (((y + 2) % NY) * 2 + core, me)
    order = z_order(nz)

    chips = [(y + 2) % NY, up, down, y]
    loads = [
        pltpu.make_async_copy(ref, to, load_sem.at[i])
        for i, (ref, to) in enumerate(
            [(left_hbm, left), (right_hbm, right), (first_hbm, first), (second_hbm, second)]
        )
    ]
    cols = [pl.ds(starts[c], widths[c]) for c in range(NC)]
    owns = [
        [
            pltpu.make_async_copy(grads.at[chips[r], core, :, :, cols[c]], own[c].at[r], own_sem.at[c, r])
            for r in range(NY)
        ]
        for c in range(NC)
    ]
    for c in range(NC):
        for r in range(NY):
            owns[c][r].start()
    for load in loads:
        load.start()

    def find_places():
        lane = lax.broadcasted_iota(jnp.int32, (8, 128), 1)
        zero = jnp.zeros((8, 128), jnp.int32)

        def step(j, carry):
            count, source, named = carry
            owner = owners[j]
            match = lane % nf == owner
            source = jnp.where(jnp.logical_and(match, count == lane // nf), j, source)
            return count + match.astype(jnp.int32), source, jnp.where(lane == j, owner, named)

        _, source, named = lax.fori_loop(0, nb, step, (zero, zero, zero))

        def earlier(i, slot):
            return slot + jnp.logical_and(named == owners[i], lane > i).astype(jnp.int32)

        table[0:8] = source
        table[8:16] = jnp.minimum(lax.fori_loop(0, nb, earlier, zero), SLOTS - 1) * nf + named
        copy = pltpu.make_async_copy(table, places, load_sem.at[4])
        copy.start()
        copy.wait()

    barrier = pltpu.get_barrier_semaphore()

    def greet(i, carry):
        for dz in order:
            p = ((x + i) % nx) * nz + (z + dz) % nz
            if dz == 0:
                @pl.when(i > 0)
                def _():
                    pl.semaphore_signal(barrier, inc=1, device_id=(d, p), device_id_type=MESH)
            else:
                pl.semaphore_signal(barrier, inc=1, device_id=(d, p), device_id_type=MESH)
        return carry

    for device in (at_pair, at_far, at_up, at_down):
        pl.semaphore_signal(barrier, inc=1, device_id=device, device_id_type=MESH)
    lax.fori_loop(0, nx, greet, 0)
    pl.semaphore_wait(barrier, nf - 1 + 4)

    def remote(source, target, send, recv, device):
        return pltpu.make_async_remote_copy(
            src_ref=source, dst_ref=target, send_sem=send, recv_sem=recv, device_id=device, device_id_type=MESH
        )

    pairs = [
        [
            remote(
                grads.at[chips[r], 1 - core, :, :, cols[c]], other[c].at[r],
                pair_send.at[c, r], pair_recv.at[c, r], at_pair,
            )
            for r in range(NY)
        ]
        for c in range(NC)
    ]
    for c in range(NC):
        for r in range(NY):
            pairs[c][r].start()

    low, high = pl.ds(0, nb // 2), pl.ds(nb // 2, nb // 2)

    def y_hop(c, i, source, target, device):
        return remote(source, target, y_send.at[c, i], y_recv.at[c, i], device)

    hops = [
        [
            y_hop(c, 0, own[c].at[0], far[c], at_far),
            y_hop(c, 1, own[c].at[1], from_down[c], at_up),
            y_hop(c, 2, own[c].at[2], from_up[c], at_down),
        ]
        if CUTS[c][1]
        else [
            y_hop(c, 0, own[c].at[0, low], far[c].at[low], at_up),
            y_hop(c, 1, own[c].at[0, high], far[c].at[high], at_down),
            y_hop(c, 2, own[c].at[1, high], from_down[c].at[high], at_up),
            y_hop(c, 3, own[c].at[2, low], from_up[c].at[low], at_down),
            y_hop(c, 4, own[c].at[1, low], from_down[c].at[low], at_up),
            y_hop(c, 5, own[c].at[2, high], from_up[c].at[high], at_down),
        ]
        for c in range(NC)
    ]
    group = min(4, nb // 2)

    def wide(ref, *at):
        return ref[at].astype(jnp.float32)

    def pair_sum(c, r):
        owns[c][r].wait()
        pairs[c][r].wait_recv()

        def step(j, carry):
            blocks = pl.ds(j * group, group)
            own[c][r, blocks] = (wide(own[c], r, blocks) + wide(other[c], r, blocks)).astype(jnp.bfloat16)
            return carry

        lax.fori_loop(0, nb // group, step, 0)

    def add_far(c, r, first_block):
        def step(j, carry):
            blocks = pl.ds(first_block + j * group, group)
            own[c][r, blocks] = (wide(own[c], r, blocks) + wide(far[c], blocks)).astype(jnp.bfloat16)
            return carry

        lax.fori_loop(0, nb // 2 // group, step, 0)

    def spread(c):
        pair_sum(c, 0)
        hops[c][0].start()
        if not CUTS[c][1]:
            hops[c][1].start()
        pair_sum(c, 1)
        hops[c][1 if CUTS[c][1] else 2].start()
        pair_sum(c, 2)
        hops[c][2 if CUTS[c][1] else 3].start()

    def forward(c):
        if CUTS[c][1]:
            return
        hops[c][0].wait_recv()
        add_far(c, 1, 0)
        hops[c][4].start()
        hops[c][1].wait_recv()
        add_far(c, 2, nb // 2)
        hops[c][5].start()

    def finish(c):
        pair_sum(c, 3)
        straight = CUTS[c][1]
        for hop in hops[c][0 if straight else 2:]:
            hop.wait_recv()

        def step(j, carry):
            blocks = pl.ds(j * group, group)
            summed = wide(own[c], 3, blocks) + wide(from_down[c], blocks) + wide(from_up[c], blocks)
            if straight:
                summed = summed + wide(far[c], blocks)
            grad[c][blocks] = summed.astype(jnp.bfloat16)
            return carry

        lax.fori_loop(0, nb // group, step, 0)

    def exchange(send, recv, at, ssem, rsem, fill_plane=None, fill=None, flat=False):
        mine = (at[0] * nf + me,) if flat else (*at, me)

        def plane(i, carry):
            px = (x + i) % nx
            if fill_plane is not None:
                fill_plane(px)
            for dz in order:
                p = px * nz + (z + dz) % nz
                if fill is not None:
                    fill(p)
                source, target = send.at[(*at, p)], recv.at[mine]
                if dz == 0:
                    @pl.when(i > 0)
                    def _():
                        remote(source, target, ssem, rsem, (d, p)).start()

                    @pl.when(i == 0)
                    def _():
                        recv[mine] = send[(*at, me)]
                else:
                    remote(source, target, ssem, rsem, (d, p)).start()
            return carry

        lax.fori_loop(0, nx, plane, 0)

    def arrived(ref, at, rsem, flat=False):
        whole = ref.at[pl.ds(at[0] * nf, nf - 1)] if flat else ref.at[(*at, pl.ds(0, nf - 1))]
        pltpu.make_async_copy(whole, whole, rsem).wait()

    def send_grad(c, stream):
        per = SLOTS if CUTS[c][2] else 1

        def fill(p):
            for i in range(per):
                g_send[c][stream, p, i] = grad[c][places[0, (stream * per + i) * nf + p]]

        exchange(g_send[c], g_recv[c], (stream,), g_ssem.at[c, stream], g_rsem.at[c, stream], fill=fill)

    streams = [range(1) if CUTS[c][2] else range(SLOTS) for c in range(NC)]
    span = nz * rows

    def product(c, s, t):
        at = (0, pl.ds(t * nz, nz), s) if CUTS[c][2] else (s, pl.ds(t * nz, nz), 0)
        held = g_recv[c][at].reshape(span, widths[c])
        return jnp.dot(held, right[s, cols[c], :], preferred_element_type=jnp.float32)

    def add_products(c, s):
        def step(t, carry):
            piece = pl.ds(t * span, span)
            made = product(c, s, t)
            if c > 0:
                made = total[s, piece] + made
            if c < NC - 1:
                total[s, piece] = made
            else:
                half[s, piece] = made.astype(jnp.bfloat16)
            return carry

        lax.fori_loop(0, nx, step, 0)

    spread(0)
    for c in range(1, NC):
        spread(c)
        if c == 1:
            find_places()
        finish(c - 1)
        for stream in streams[c - 1]:
            send_grad(c - 1, stream)
        forward(c)
    for load in loads:
        load.wait()
    for s in range(SLOTS):
        for t in range(nx):
            piece = pl.ds(t * nz * rows, nz * rows)
            left_t[s, :, piece] = left[s, piece, :].T
    finish(NC - 1)
    for stream in streams[NC - 1]:
        send_grad(NC - 1, stream)

    for c in range(NC - 1):
        for stream in streams[c]:
            arrived(g_recv[c], (stream,), g_rsem.at[c, stream])
        for s in range(SLOTS):
            add_products(c, s)

    for s in range(SLOTS):
        if s < len(streams[NC - 1]):
            arrived(g_recv[NC - 1], (s,), g_rsem.at[NC - 1, s])
        add_products(NC - 1, s)

        def rotate(px, s=s):
            made = jnp.dot(left_t[s, pl.ds(px * span, span)], half[s], preferred_element_type=jnp.float32)
            r_send[s, pl.ds(px * nz, nz)] = made.astype(jnp.bfloat16).reshape(nz, rows, columns)

        exchange(r_send, r_recv, (s,), r_ssem.at[s], r_rsem.at[s], fill_plane=rotate, flat=True)

    for s in range(SLOTS):
        arrived(r_recv, (s,), r_rsem.at[s], flat=True)

        def direct(p, s=s):
            block = places[0, s * nf + p]
            first_wide, second_wide = adam(r_recv[s * nf + p], first[block], second[block])
            d_send[s, p] = (first_wide / (jnp.sqrt(second_wide) + EPSILON)).astype(jnp.bfloat16)

        exchange(d_send, d_recv, (s,), d_ssem.at[s], d_rsem.at[s], fill=direct)

    def moments(j, carry):
        first_wide, second_wide = adam(r_recv[places[8, j]], first[j], second[j])
        first_new[j] = first_wide.astype(jnp.bfloat16)
        second_new[j] = second_wide
        return carry

    lax.fori_loop(0, nb, moments, 0)
    outs = [
        pltpu.make_async_copy(ref, to, out_sem.at[i])
        for i, (ref, to) in enumerate([(first_new, first_out), (second_new, second_out), (update, update_out)])
    ]
    outs[0].start()
    outs[1].start()

    for s in range(SLOTS):
        arrived(d_recv, (s,), d_rsem.at[s])

        def undo_right(t, carry, s=s):
            held = d_recv[s, pl.ds(t * nz, nz)].reshape(span, columns)
            made = lax.dot_general(held, right[s], (((1,), (1,)), ((), ())), preferred_element_type=jnp.float32)
            back[s, pl.ds(t * span, span)] = made.astype(jnp.bfloat16)
            return carry

        lax.fori_loop(0, nx, undo_right, 0)

        def undo_left(px, s=s):
            made = jnp.dot(left[s, pl.ds(px * span, span)], back[s], preferred_element_type=jnp.float32)
            u_send[s, pl.ds(px * nz, nz)] = made.astype(jnp.bfloat16).reshape(nz, rows, columns)

        exchange(u_send, u_recv, (s,), u_ssem.at[s], u_rsem.at[s], fill_plane=undo_left, flat=True)

    for s in range(SLOTS):
        arrived(u_recv, (s,), u_rsem.at[s], flat=True)

    def pick(j, carry):
        update[j] = u_recv[places[8, j]]
        return carry

    lax.fori_loop(0, nb, pick, 0)
    outs[2].start()

    for c in range(NC):
        for r in range(NY):
            pairs[c][r].wait_send()
        for hop in hops[c]:
            hop.wait_send()
        for s in streams[c]:
            arrived(g_send[c], (s,), g_ssem.at[c, s])
    for s in range(SLOTS):
        arrived(r_send, (s,), r_ssem.at[s])
        arrived(d_send, (s,), d_ssem.at[s])
        arrived(u_send, (s,), u_ssem.at[s])
    for out in outs:
        out.wait()


def per_device(nx, nz, grad_parts, first_moment, second_moment, left_basis, right_basis, owner_list):
    nf = nx * nz
    nb, rows, columns = first_moment.shape
    grads = grad_parts.reshape(NY, 2, nb, rows, columns)
    bf16, f32 = jnp.bfloat16, jnp.float32
    dma = pltpu.SemaphoreType.DMA
    order = nf * rows
    moved = pltpu.VMEM((SLOTS, nf, rows, columns), bf16)
    flat = pltpu.VMEM((SLOTS * nf, rows, columns), bf16)
    square = pltpu.VMEM((SLOTS, order, columns), bf16)
    hbm = pl.BlockSpec(memory_space=pl.ANY)
    smem = pl.BlockSpec(memory_space=pltpu.SMEM)
    cut_scratch = []
    for (_, _, merged), width in zip(CUTS, column_cuts(columns)[1]):
        part = pltpu.VMEM((NY, nb, rows, width), bf16)
        group = pltpu.VMEM((nb, rows, width), bf16)
        per = SLOTS if merged else 1
        sent = pltpu.VMEM((SLOTS // per, nf, per, rows, width), bf16)
        cut_scratch += [part, part, group, group, group, group, sent, sent]
    return pl.pallas_call(
        functools.partial(kernel, nx, nz),
        out_shape=(
            jax.ShapeDtypeStruct((nb, rows, columns), bf16),
            jax.ShapeDtypeStruct((nb, rows, columns), f32),
            jax.ShapeDtypeStruct((nb, rows, columns), bf16),
        ),
        in_specs=[smem, hbm, hbm, hbm, hbm, hbm],
        out_specs=(hbm, hbm, hbm),
        scratch_shapes=cut_scratch + [
            pltpu.VMEM((16, 128), jnp.int32), pltpu.SMEM((16, 128), jnp.int32),
            moved, flat, moved, moved, moved, flat,
            pltpu.VMEM((nb, rows, columns), bf16),
            pltpu.VMEM((nb, rows, columns), f32),
            square, square, square,
            pltpu.VMEM((SLOTS, order, columns), f32),
            square, square,
            pltpu.VMEM((nb, rows, columns), bf16),
            pltpu.VMEM((nb, rows, columns), f32),
            pltpu.VMEM((nb, rows, columns), bf16),
            dma((5,)), dma((NC, NY)), dma((NC, NY)), dma((NC, NY)), dma((NC, 6)), dma((NC, 6)),
            dma((NC, SLOTS)), dma((NC, SLOTS)),
            dma((SLOTS,)), dma((SLOTS,)), dma((SLOTS,)), dma((SLOTS,)), dma((SLOTS,)), dma((SLOTS,)),
            dma((3,)),
        ],
        compiler_params=pltpu.CompilerParams(
            collective_id=0, has_side_effects=True, vmem_limit_bytes=VMEM_BYTES
        ),
        cost_estimate=pl.CostEstimate(
            flops=SLOTS * 8 * order * columns * columns, bytes_accessed=16 * 1024 * 1024, transcendentals=0
        ),
    )(
        owner_list.reshape(nb), grads, first_moment, second_moment,
        left_basis.reshape(SLOTS, order, order), right_basis.reshape(SLOTS, columns, columns),
    )


def solution(mesh):
    nf = mesh.shape["fsdp"]
    nz = min(8, nf // 2)
    placed = (
        P("dp", None, "fsdp", None),
        P("dp", "fsdp", None),
        P("dp", "fsdp", None),
        P("dp", "fsdp", None, None, None),
        P("dp", "fsdp", None, None, None),
        P("dp", None, None),
    )
    return jax.shard_map(
        functools.partial(per_device, nf // nz, nz),
        mesh=mesh,
        in_specs=placed,
        out_specs=(P("dp", "fsdp", None), P("dp", "fsdp", None), P("dp", "fsdp", None)),
        check_vma=False,
    )
```

time: 129 us -> 125 us (0.969); the launches traced: 127 us -> 124 us
  other arithmetic: 1.67 us -> 0 us
    unnamed x11 -> x3, local copies, waits for them, and re-layouts: 7.27 us -> 6.04 us
where the time goes in v2:
time: 125 us; the launch traced here: 124 us
  Pallas kernels  118 us (94%)
  local copies, waits for them, and re-layouts  6.04 us (5%)
    pallas_call x1, Pallas kernels, per_device(): pl.pallas_call(functools.partial(kernel, nx, nz), out_shape=(jax.ShapeDty...  118 us
    unnamed x3, local copies, waits for them, and re-layouts  6.04 us

profile of v2, /device:TPU:8, one launch (start us, length us, event | category | flops | bytes accessed | tf_op | source)
XLA Modules:
  0.0 124.3 jit_solution(2753965200017069719)
XLA Ops:
  0.6 117.6 %shard_map.85 = (bf16[32,16,512]{2,1,0:T(8,128)(2,1)}, f32[32,16,512]{2,1,0:T(8,128)}, bf16[32,16,512]{2,1,0:T(8,128)(2,1)}) custom-call(s32[32]{0:T(128)} %bitcast.7, bf16[4,2,32,16,512]{4,3,2,1,0:T(8,128)(2,1)} %bitcast.4, bf16[32,16,512]{2,1,0:T(8,128)(2,1)} %first_hbm.1, f32[32,16,512]{2,1,0:T(8,128)} %second_hbm.1, bf16[2,512,512]{2,1,0:T(8,128)(2,1)} %bitcast.5, ...), custom_call_target="tpu_custom_call" | custom-call | flops 2147483648 | bytes 16777216 | tf_op jit(solution)/shard_map/pallas_call | solution.py:413
  118.2 1.9 %copy.12 = bf16[32,16,512]{2,1,0:T(8,128)(2,1)} copy(bf16[32,16,512]{2,1,0:T(8,128)(2,1)} %get-tuple-element.6) | data formatting | bytes 1048576
  120.1 2.3 %copy.13 = f32[32,16,512]{2,1,0:T(8,128)} copy(f32[32,16,512]{2,1,0:T(8,128)} %get-tuple-element.7) | data formatting | bytes 2097152
  122.4 1.9 %copy.14 = bf16[32,16,512]{2,1,0:T(8,128)(2,1)} copy(bf16[32,16,512]{2,1,0:T(8,128)(2,1)} %get-tuple-element.8) | data formatting | bytes 1048576

commit v3 on v2

--- a/solution.py
+++ b/solution.py
@@ -12,10 +12,10 @@
 EPSILON = 1e-08
 
 MESH = pl.DeviceIdType.MESH
-VMEM_BYTES = 60 * 1024 * 1024
+VMEM_BYTES = 32 * 1024 * 1024
 NY = 4
 SLOTS = 2
-CUTS = ((2, True, True), (2, False, True), (4, False, False))
+CUTS = ((2, True, True), (2, False, True), (2, False, True), (2, False, False))
 NC = len(CUTS)
 
 
@@ -43,17 +43,17 @@
 def kernel(
     nx, nz,
     owners, grads, first_hbm, second_hbm, left_hbm, right_hbm,
-    first_out, second_out, update_out,
+    first_new, second_new, u_recv, table,
     *scratch,
 ):
     cut_refs = [scratch[c * 8:c * 8 + 8] for c in range(NC)]
     own, other, far, from_down, from_up, grad, g_send, g_recv = zip(*cut_refs)
     (
-        table, places,
-        r_send, r_recv, d_send, d_recv, u_send, u_recv,
-        first, second, left, right, left_t, total, half, back, first_new, second_new, update,
+        places,
+        r_send, r_recv, d_send, d_recv, u_send,
+        first, second, left, right, left_t, total, half, back,
         load_sem, own_sem, pair_send, pair_recv, y_send, y_recv,
-        g_ssem, g_rsem, r_ssem, r_rsem, d_ssem, d_rsem, u_ssem, u_rsem, out_sem,
+        g_ssem, g_rsem, r_ssem, r_rsem, d_ssem, d_rsem, u_ssem, u_rsem,
     ) = scratch[NC * 8:]
     nf = nx * nz
     nb, rows, columns = first.shape
@@ -81,11 +81,8 @@
         ]
         for c in range(NC)
     ]
-    for c in range(NC):
-        for r in range(NY):
-            owns[c][r].start()
-    for load in loads:
-        load.start()
+    for r in range(NY):
+        owns[0][r].start()
 
     def find_places():
         lane = lax.broadcasted_iota(jnp.int32, (8, 128), 1)
@@ -145,6 +142,10 @@
     for c in range(NC):
         for r in range(NY):
             pairs[c][r].start()
+            if c > 0:
+                owns[c][r].start()
+    for load in loads:
+        load.start()
 
     low, high = pl.ds(0, nb // 2), pl.ds(nb // 2, nb // 2)
 
@@ -298,15 +299,16 @@
         for stream in streams[c - 1]:
             send_grad(c - 1, stream)
         forward(c)
+    finish(NC - 1)
+    for stream in streams[NC - 1]:
+        send_grad(NC - 1, stream)
+
     for load in loads:
         load.wait()
     for s in range(SLOTS):
         for t in range(nx):
             piece = pl.ds(t * nz * rows, nz * rows)
             left_t[s, :, piece] = left[s, piece, :].T
-    finish(NC - 1)
-    for stream in streams[NC - 1]:
-        send_grad(NC - 1, stream)
 
     for c in range(NC - 1):
         for stream in streams[c]:
@@ -342,13 +344,6 @@
         return carry
 
     lax.fori_loop(0, nb, moments, 0)
-    outs = [
-        pltpu.make_async_copy(ref, to, out_sem.at[i])
-        for i, (ref, to) in enumerate([(first_new, first_out), (second_new, second_out), (update, update_out)])
-    ]
-    outs[0].start()
-    outs[1].start()
-
     for s in range(SLOTS):
         arrived(d_recv, (s,), d_rsem.at[s])
 
@@ -368,13 +363,6 @@
 
     for s in range(SLOTS):
         arrived(u_recv, (s,), u_rsem.at[s], flat=True)
-
-    def pick(j, carry):
-        update[j] = u_recv[places[8, j]]
-        return carry
-
-    lax.fori_loop(0, nb, pick, 0)
-    outs[2].start()
 
     for c in range(NC):
         for r in range(NY):
@@ -387,8 +375,24 @@
         arrived(r_send, (s,), r_ssem.at[s])
         arrived(d_send, (s,), d_ssem.at[s])
         arrived(u_send, (s,), u_ssem.at[s])
+
+
+def deliver(places, first_new, second_new, u_recv, first_out, second_out, update_out, sem):
+    outs = [
+        pltpu.make_async_copy(first_new, first_out, sem.at[0]),
+        pltpu.make_async_copy(second_new, second_out, sem.at[1]),
+    ]
+    for out in outs:
+        out.start()
+
+    def pick(j, carry):
+        pltpu.make_async_copy(u_recv.at[places[8, j]], update_out.at[j], sem.at[2]).start()
+        return carry
+
+    lax.fori_loop(0, update_out.shape[0], pick, 0)
     for out in outs:
         out.wait()
+    pltpu.make_async_copy(update_out, update_out, sem.at[2]).wait()
 
 
 def per_device(nx, nz, grad_parts, first_moment, second_moment, left_basis, right_basis, owner_list):
@@ -410,30 +414,32 @@
         per = SLOTS if merged else 1
         sent = pltpu.VMEM((SLOTS // per, nf, per, rows, width), bf16)
         cut_scratch += [part, part, group, group, group, group, sent, sent]
-    return pl.pallas_call(
+    vmem = pl.BlockSpec(memory_space=pltpu.VMEM)
+
+    def stay(array):
+        return pltpu.with_memory_space_constraint(array, pltpu.HBM)
+
+    first_new, second_new, u_recv, table = pl.pallas_call(
         functools.partial(kernel, nx, nz),
         out_shape=(
-            jax.ShapeDtypeStruct((nb, rows, columns), bf16),
-            jax.ShapeDtypeStruct((nb, rows, columns), f32),
-            jax.ShapeDtypeStruct((nb, rows, columns), bf16),
+            pltpu.VMEM((nb, rows, columns), bf16),
+            pltpu.VMEM((nb, rows, columns), f32),
+            pltpu.VMEM((SLOTS * nf, rows, columns), bf16),
+            pltpu.VMEM((16, 128), jnp.int32),
         ),
         in_specs=[smem, hbm, hbm, hbm, hbm, hbm],
-        out_specs=(hbm, hbm, hbm),
+        out_specs=(vmem, vmem, vmem, vmem),
         scratch_shapes=cut_scratch + [
-            pltpu.VMEM((16, 128), jnp.int32), pltpu.SMEM((16, 128), jnp.int32),
-            moved, flat, moved, moved, moved, flat,
+            pltpu.SMEM((16, 128), jnp.int32),
+            moved, flat, moved, moved, moved,
             pltpu.VMEM((nb, rows, columns), bf16),
             pltpu.VMEM((nb, rows, columns), f32),
             square, square, square,
             pltpu.VMEM((SLOTS, order, columns), f32),
             square, square,
-            pltpu.VMEM((nb, rows, columns), bf16),
-            pltpu.VMEM((nb, rows, columns), f32),
-            pltpu.VMEM((nb, rows, columns), bf16),
             dma((5,)), dma((NC, NY)), dma((NC, NY)), dma((NC, NY)), dma((NC, 6)), dma((NC, 6)),
             dma((NC, SLOTS)), dma((NC, SLOTS)),
             dma((SLOTS,)), dma((SLOTS,)), dma((SLOTS,)), dma((SLOTS,)), dma((SLOTS,)), dma((SLOTS,)),
-            dma((3,)),
         ],
         compiler_params=pltpu.CompilerParams(
             collective_id=0, has_side_effects=True, vmem_limit_bytes=VMEM_BYTES
@@ -442,9 +448,20 @@
             flops=SLOTS * 8 * order * columns * columns, bytes_accessed=16 * 1024 * 1024, transcendentals=0
         ),
     )(
-        owner_list.reshape(nb), grads, first_moment, second_moment,
-        left_basis.reshape(SLOTS, order, order), right_basis.reshape(SLOTS, columns, columns),
+        stay(owner_list.reshape(nb)), stay(grads), stay(first_moment), stay(second_moment),
+        stay(left_basis.reshape(SLOTS, order, order)), stay(right_basis.reshape(SLOTS, columns, columns)),
     )
+    return pl.pallas_call(
+        deliver,
+        out_shape=(
+            jax.ShapeDtypeStruct((nb, rows, columns), bf16),
+            jax.ShapeDtypeStruct((nb, rows, columns), f32),
+            jax.ShapeDtypeStruct((nb, rows, columns), bf16),
+        ),
+        in_specs=[smem, vmem, vmem, vmem],
+        out_specs=(hbm, hbm, hbm),
+        scratch_shapes=[dma((3,))],
+    )(table, first_new, second_new, u_recv)
 
 
 def solution(mesh):

time: 125 us -> 126 us (level); the launches traced: 124 us -> 124 us
  local copies, waits for them, and re-layouts: 6.04 us -> 3.35 us
  Pallas kernels: 118 us -> 120 us
    unnamed x3 -> x8, local copies, waits for them, and re-layouts: 6.04 us -> 3.35 us
    pallas_call x1 -> x2, Pallas kernels: 118 us -> 120 us  [the longest x1 117 us: per_device(): pl.pallas_call(functools.partial(kernel, nx, nz), out_shape=(pltpu.VMEM((...]
where the time goes in v3:
time: 126 us; the launch traced here: 124 us
  Pallas kernels  120 us (95%)
  local copies, waits for them, and re-layouts  3.35 us (3%)
    pallas_call x1, Pallas kernels, per_device(): pl.pallas_call(functools.partial(kernel, nx, nz), out_shape=(pltpu.VMEM((...  117 us
    unnamed x8, local copies, waits for them, and re-layouts  3.35 us
    pallas_call x1, Pallas kernels, per_device(): pl.pallas_call(deliver, out_shape=(jax.ShapeDtypeStruct((nb, rows, column...  3.02 us

profile of v3, /device:TPU:8, one launch (start us, length us, event | category | flops | bytes accessed | tf_op | source)
XLA Modules:
  0.0 123.9 jit_solution(10124290105077717453)
XLA Ops:
  0.6 116.9 %shard_map.85 = (bf16[32,16,512]{2,1,0:T(8,128)(2,1)S(1)}, f32[32,16,512]{2,1,0:T(8,128)S(1)}, bf16[64,16,512]{2,1,0:T(8,128)(2,1)S(1)}, s32[16,128]{1,0:T(8,128)S(1)}) custom-call(s32[32]{0:T(128)} %bitcast.7, bf16[4,2,32,16,512]{4,3,2,1,0:T(8,128)(2,1)} %bitcast.4, bf16[32,16,512]{2,1,0:T(8,128)(2,1)} %first_hbm.1, f32[32,16,512]{2,1,0:T(8,128)} %second_hbm.1, ...), custom_call_target="tpu_custom_call" | custom-call | flops 2147483648 | bytes 16777216 | tf_op jit(solution)/shard_map/pallas_call | solution.py:422
  117.5 0.0 copy-start
  117.5 1.0 copy-done
  118.5 0.0 copy-start.1
  118.5 1.0 copy-done.1
  119.5 0.0 copy-start.2
  119.5 0.8 copy-done.2
  120.3 0.0 copy-start.3
  120.3 0.6 copy-done.3
  120.9 3.0 %shard_map.86 = (bf16[32,16,512]{2,1,0:T(8,128)(2,1)}, f32[32,16,512]{2,1,0:T(8,128)}, bf16[32,16,512]{2,1,0:T(8,128)(2,1)}) custom-call(s32[16,128]{1,0:T(8,128)} %copy-done.3, bf16[32,16,512]{2,1,0:T(8,128)(2,1)} %copy-done.2, f32[32,16,512]{2,1,0:T(8,128)} %copy-done, bf16[64,16,512]{2,1,0:T(8,128)(2,1)} %copy-done.1), custom_call_target="tpu_custom_call" | custom-call | tf_op jit(solution)/shard_map/pallas_call | solution.py:454
Async XLA Ops:
  117.5 1.0 copy-start
  118.5 1.0 copy-start.1
  119.5 0.8 copy-start.2
  120.3 0.6 copy-start.3

commit v4 on v3

--- a/solution.py
+++ b/solution.py
@@ -13,9 +13,10 @@
 
 MESH = pl.DeviceIdType.MESH
 VMEM_BYTES = 32 * 1024 * 1024
+DELIVER_VMEM_BYTES = 8 * 1024 * 1024
 NY = 4
 SLOTS = 2
-CUTS = ((2, True, True), (2, False, True), (2, False, True), (2, False, False))
+CUTS = ((2, False, True), (2, False, True), (2, False, True), (2, False, False))
 NC = len(CUTS)
 
 
@@ -30,7 +31,7 @@
         order.append(step)
         if nz - step != step:
             order.append(nz - step)
-    return order
+    return order[::-1]
 
 
 def adam(rotated, first, second):
@@ -43,14 +44,14 @@
 def kernel(
     nx, nz,
     owners, grads, first_hbm, second_hbm, left_hbm, right_hbm,
-    first_new, second_new, u_recv, table,
+    first_new, second_new, update,
     *scratch,
 ):
     cut_refs = [scratch[c * 8:c * 8 + 8] for c in range(NC)]
     own, other, far, from_down, from_up, grad, g_send, g_recv = zip(*cut_refs)
     (
-        places,
-        r_send, r_recv, d_send, d_recv, u_send,
+        table, named_blocks, places,
+        r_send, r_recv, d_send, d_recv, u_send, u_recv,
         first, second, left, right, left_t, total, half, back,
         load_sem, own_sem, pair_send, pair_recv, y_send, y_recv,
         g_ssem, g_rsem, r_ssem, r_rsem, d_ssem, d_rsem, u_ssem, u_rsem,
@@ -81,16 +82,19 @@
         ]
         for c in range(NC)
     ]
+    owner_load = pltpu.make_async_copy(owners, named_blocks, load_sem.at[5])
+    owner_load.start()
     for r in range(NY):
         owns[0][r].start()
 
     def find_places():
+        owner_load.wait()
         lane = lax.broadcasted_iota(jnp.int32, (8, 128), 1)
         zero = jnp.zeros((8, 128), jnp.int32)
 
         def step(j, carry):
             count, source, named = carry
-            owner = owners[j]
+            owner = named_blocks[j]
             match = lane % nf == owner
             source = jnp.where(jnp.logical_and(match, count == lane // nf), j, source)
             return count + match.astype(jnp.int32), source, jnp.where(lane == j, owner, named)
@@ -98,7 +102,7 @@
         _, source, named = lax.fori_loop(0, nb, step, (zero, zero, zero))
 
         def earlier(i, slot):
-            return slot + jnp.logical_and(named == owners[i], lane > i).astype(jnp.int32)
+            return slot + jnp.logical_and(named == named_blocks[i], lane > i).astype(jnp.int32)
 
         table[0:8] = source
         table[8:16] = jnp.minimum(lax.fori_loop(0, nb, earlier, zero), SLOTS - 1) * nf + named
@@ -233,7 +237,7 @@
         mine = (at[0] * nf + me,) if flat else (*at, me)
 
         def plane(i, carry):
-            px = (x + i) % nx
+            px = (x + nx // 2 + i) % nx
             if fill_plane is not None:
                 fill_plane(px)
             for dz in order:
@@ -242,11 +246,11 @@
                     fill(p)
                 source, target = send.at[(*at, p)], recv.at[mine]
                 if dz == 0:
-                    @pl.when(i > 0)
+                    @pl.when(i != nx - nx // 2)
                     def _():
                         remote(source, target, ssem, rsem, (d, p)).start()
 
-                    @pl.when(i == 0)
+                    @pl.when(i == nx - nx // 2)
                     def _():
                         recv[mine] = send[(*at, me)]
                 else:
@@ -292,13 +296,14 @@
 
     spread(0)
     for c in range(1, NC):
-        spread(c)
         if c == 1:
             find_places()
+        forward(c - 1)
+        spread(c)
         finish(c - 1)
         for stream in streams[c - 1]:
             send_grad(c - 1, stream)
-        forward(c)
+    forward(NC - 1)
     finish(NC - 1)
     for stream in streams[NC - 1]:
         send_grad(NC - 1, stream)
@@ -363,6 +368,12 @@
 
     for s in range(SLOTS):
         arrived(u_recv, (s,), u_rsem.at[s], flat=True)
+
+    def pick(j, carry):
+        update[j] = u_recv[places[8, j]]
+        return carry
+
+    lax.fori_loop(0, nb, pick, 0)
 
     for c in range(NC):
         for r in range(NY):
@@ -377,22 +388,13 @@
         arrived(u_send, (s,), u_ssem.at[s])
 
 
-def deliver(places, first_new, second_new, u_recv, first_out, second_out, update_out, sem):
-    outs = [
-        pltpu.make_async_copy(first_new, first_out, sem.at[0]),
-        pltpu.make_async_copy(second_new, second_out, sem.at[1]),
-    ]
-    for out in outs:
-        out.start()
-
-    def pick(j, carry):
-        pltpu.make_async_copy(u_recv.at[places[8, j]], update_out.at[j], sem.at[2]).start()
-        return carry
-
-    lax.fori_loop(0, update_out.shape[0], pick, 0)
-    for out in outs:
-        out.wait()
-    pltpu.make_async_copy(update_out, update_out, sem.at[2]).wait()
+def deliver(*refs):
+    count = (len(refs) - 1) // 2
+    copies = [pltpu.make_async_copy(refs[i], refs[count + i], refs[-1].at[i]) for i in range(count)]
+    for copy in copies:
+        copy.start()
+    for copy in copies:
+        copy.wait()
 
 
 def per_device(nx, nz, grad_parts, first_moment, second_moment, left_basis, right_basis, owner_list):
@@ -406,7 +408,6 @@
     flat = pltpu.VMEM((SLOTS * nf, rows, columns), bf16)
     square = pltpu.VMEM((SLOTS, order, columns), bf16)
     hbm = pl.BlockSpec(memory_space=pl.ANY)
-    smem = pl.BlockSpec(memory_space=pltpu.SMEM)
     cut_scratch = []
     for (_, _, merged), width in zip(CUTS, column_cuts(columns)[1]):
         part = pltpu.VMEM((NY, nb, rows, width), bf16)
@@ -419,25 +420,24 @@
     def stay(array):
         return pltpu.with_memory_space_constraint(array, pltpu.HBM)
 
-    first_new, second_new, u_recv, table = pl.pallas_call(
+    made = pl.pallas_call(
         functools.partial(kernel, nx, nz),
         out_shape=(
             pltpu.VMEM((nb, rows, columns), bf16),
             pltpu.VMEM((nb, rows, columns), f32),
-            pltpu.VMEM((SLOTS * nf, rows, columns), bf16),
-            pltpu.VMEM((16, 128), jnp.int32),
+            pltpu.VMEM((nb, rows, columns), bf16),
         ),
-        in_specs=[smem, hbm, hbm, hbm, hbm, hbm],
-        out_specs=(vmem, vmem, vmem, vmem),
+        in_specs=[hbm, hbm, hbm, hbm, hbm, hbm],
+        out_specs=(vmem, vmem, vmem),
         scratch_shapes=cut_scratch + [
-            pltpu.SMEM((16, 128), jnp.int32),
-            moved, flat, moved, moved, moved,
+            pltpu.VMEM((16, 128), jnp.int32), pltpu.SMEM((nb,), jnp.int32), pltpu.SMEM((16, 128), jnp.int32),
+            moved, flat, moved, moved, moved, flat,
             pltpu.VMEM((nb, rows, columns), bf16),
             pltpu.VMEM((nb, rows, columns), f32),
             square, square, square,
             pltpu.VMEM((SLOTS, order, columns), f32),
             square, square,
-            dma((5,)), dma((NC, NY)), dma((NC, NY)), dma((NC, NY)), dma((NC, 6)), dma((NC, 6)),
+            dma((6,)), dma((NC, NY)), dma((NC, NY)), dma((NC, NY)), dma((NC, 6)), dma((NC, 6)),
             dma((NC, SLOTS)), dma((NC, SLOTS)),
             dma((SLOTS,)), dma((SLOTS,)), dma((SLOTS,)), dma((SLOTS,)), dma((SLOTS,)), dma((SLOTS,)),
         ],
@@ -458,10 +458,11 @@
             jax.ShapeDtypeStruct((nb, rows, columns), f32),
             jax.ShapeDtypeStruct((nb, rows, columns), bf16),
         ),
-        in_specs=[smem, vmem, vmem, vmem],
+        in_specs=[vmem, vmem, vmem],
         out_specs=(hbm, hbm, hbm),
         scratch_shapes=[dma((3,))],
-    )(table, first_new, second_new, u_recv)
+        compiler_params=pltpu.CompilerParams(vmem_limit_bytes=DELIVER_VMEM_BYTES),
+    )(*(pltpu.with_memory_space_constraint(array, pltpu.VMEM) for array in made))
 
 
 def solution(mesh):

time: 126 us -> 118 us (0.937); the launches traced: 124 us -> 117 us
  local copies, waits for them, and re-layouts: 3.35 us -> 0 us
  Pallas kernels: 120 us -> 117 us
    unnamed x8 -> x0, local copies, waits for them, and re-layouts: 3.35 us -> none
    pallas_call x1, Pallas kernels: 3.02 us -> 1.34 us  [per_device(): pl.pallas_call(deliver, out_shape=(jax.ShapeDtypeStruct((nb, rows, column...]
    pallas_call x1, Pallas kernels: 117 us -> 115 us  [per_device(): pl.pallas_call(functools.partial(kernel, nx, nz), out_shape=(pltpu.VMEM((...]
where the time goes in v4:
time: 118 us; the launch traced here: 117 us
  Pallas kernels  117 us (99%)
    pallas_call x1, Pallas kernels, per_device(): pl.pallas_call(functools.partial(kernel, nx, nz), out_shape=(pltpu.VMEM((...  115 us

profile of v4, /device:TPU:8, one launch (start us, length us, event | category | flops | bytes accessed | tf_op | source)
XLA Modules:
  0.0 117.4 jit_solution(4170275724543494622)
XLA Ops:
  0.6 115.4 %shard_map.85 = (bf16[32,16,512]{2,1,0:T(8,128)(2,1)S(1)}, f32[32,16,512]{2,1,0:T(8,128)S(1)}, bf16[32,16,512]{2,1,0:T(8,128)(2,1)S(1)}) custom-call(s32[32]{0:T(128)} %bitcast.7, bf16[4,2,32,16,512]{4,3,2,1,0:T(8,128)(2,1)} %bitcast.4, bf16[32,16,512]{2,1,0:T(8,128)(2,1)} %first_hbm.1, f32[32,16,512]{2,1,0:T(8,128)} %second_hbm.1, ...), custom_call_target="tpu_custom_call" | custom-call | flops 2147483648 | bytes 16777216 | tf_op jit(solution)/shard_map/pallas_call | solution.py:423
  116.1 1.3 %shard_map.86 = (bf16[32,16,512]{2,1,0:T(8,128)(2,1)}, f32[32,16,512]{2,1,0:T(8,128)}, bf16[32,16,512]{2,1,0:T(8,128)(2,1)}) custom-call(bf16[32,16,512]{2,1,0:T(8,128)(2,1)S(1)} %get-tuple-element.6.refs_0_, f32[32,16,512]{2,1,0:T(8,128)S(1)} %get-tuple-element.7.refs_1_, bf16[32,16,512]{2,1,0:T(8,128)(2,1)S(1)} %get-tuple-element.8.refs_2_), custom_call_target="tpu_custom_call" | custom-call | tf_op jit(solution)/shard_map/pallas_call | solution.py:454

commit v5 on v4

--- a/solution.py
+++ b/solution.py
@@ -54,7 +54,7 @@
         r_send, r_recv, d_send, d_recv, u_send, u_recv,
         first, second, left, right, left_t, total, half, back,
         load_sem, own_sem, pair_send, pair_recv, y_send, y_recv,
-        g_ssem, g_rsem, r_ssem, r_rsem, d_ssem, d_rsem, u_ssem, u_rsem,
+        g_ssem, g_rsem, r_ssem, r_rsem, d_ssem, d_rsem, u_ssem, u_rsem, round_sem,
     ) = scratch[NC * 8:]
     nf = nx * nz
     nb, rows, columns = first.shape
@@ -112,21 +112,30 @@
 
     barrier = pltpu.get_barrier_semaphore()
 
-    def greet(i, carry):
-        for dz in order:
-            p = ((x + i) % nx) * nz + (z + dz) % nz
-            if dz == 0:
-                @pl.when(i > 0)
-                def _():
-                    pl.semaphore_signal(barrier, inc=1, device_id=(d, p), device_id_type=MESH)
-            else:
-                pl.semaphore_signal(barrier, inc=1, device_id=(d, p), device_id_type=MESH)
-        return carry
-
-    for device in (at_pair, at_far, at_up, at_down):
+    def across(dx, dz):
+        return d, ((x + nx + dx) % nx) * nz + (z + nz + dz) % nz
+
+    near = [at_pair, at_far, at_up, at_down, across(0, 1), across(0, -1), across(1, 0), across(-1, 0)]
+    for device in near:
         pl.semaphore_signal(barrier, inc=1, device_id=device, device_id_type=MESH)
-    lax.fori_loop(0, nx, greet, 0)
-    pl.semaphore_wait(barrier, nf - 1 + 4)
+    pl.semaphore_wait(barrier, len(near))
+
+    rounds = [[(0, 1), (0, -1)], [(0, 2), (0, -2)]] if nz > 2 else []
+    rounds.append([(1, 0), (-1, 0)])
+    if nx > 2:
+        rounds.append([(2, 0)])
+
+    def tell(k):
+        for dx, dz in rounds[k]:
+            pl.semaphore_signal(round_sem.at[k], inc=1, device_id=across(dx, dz), device_id_type=MESH)
+
+    def hear(k):
+        if k < len(rounds):
+            pl.semaphore_wait(round_sem.at[k], len(rounds[k]))
+            if k + 1 < len(rounds):
+                tell(k + 1)
+
+    tell(0)
 
     def remote(source, target, send, recv, device):
         return pltpu.make_async_remote_copy(
@@ -294,11 +303,16 @@
 
         lax.fori_loop(0, nx, step, 0)
 
+    hear(0)
     spread(0)
     for c in range(1, NC):
         if c == 1:
+            hear(1)
             find_places()
+            hear(2)
         forward(c - 1)
+        if c == 1:
+            hear(3)
         spread(c)
         finish(c - 1)
         for stream in streams[c - 1]:
@@ -440,6 +454,7 @@
             dma((6,)), dma((NC, NY)), dma((NC, NY)), dma((NC, NY)), dma((NC, 6)), dma((NC, 6)),
             dma((NC, SLOTS)), dma((NC, SLOTS)),
             dma((SLOTS,)), dma((SLOTS,)), dma((SLOTS,)), dma((SLOTS,)), dma((SLOTS,)), dma((SLOTS,)),
+            pltpu.SemaphoreType.REGULAR((4,)),
         ],
         compiler_params=pltpu.CompilerParams(
             collective_id=0, has_side_effects=True, vmem_limit_bytes=VMEM_BYTES

time: 118 us -> 113 us (0.958)
  Pallas kernels: 117 us -> 112 us
    pallas_call x1, Pallas kernels: 115 us -> 111 us  [per_device(): pl.pallas_call(functools.partial(kernel, nx, nz), out_shape=(pltpu.VMEM((...]
where the time goes in v5:
time: 113 us
  Pallas kernels  112 us (99%)
    pallas_call x1, Pallas kernels, per_device(): pl.pallas_call(functools.partial(kernel, nx, nz), out_shape=(pltpu.VMEM((...  111 us

profile of v5, /device:TPU:8, one launch (start us, length us, event | category | flops | bytes accessed | tf_op | source)
XLA Modules:
  0.0 113.0 jit_solution(9532424609364042773)
XLA Ops:
  0.6 111.0 %shard_map.85 = (bf16[32,16,512]{2,1,0:T(8,128)(2,1)S(1)}, f32[32,16,512]{2,1,0:T(8,128)S(1)}, bf16[32,16,512]{2,1,0:T(8,128)(2,1)S(1)}) custom-call(s32[32]{0:T(128)} %bitcast.7, bf16[4,2,32,16,512]{4,3,2,1,0:T(8,128)(2,1)} %bitcast.4, bf16[32,16,512]{2,1,0:T(8,128)(2,1)} %first_hbm.1, f32[32,16,512]{2,1,0:T(8,128)} %second_hbm.1, ...), custom_call_target="tpu_custom_call" | custom-call | flops 2147483648 | bytes 16777216 | tf_op jit(solution)/shard_map/pallas_call | solution.py:437
  111.6 1.3 %shard_map.86 = (bf16[32,16,512]{2,1,0:T(8,128)(2,1)}, f32[32,16,512]{2,1,0:T(8,128)}, bf16[32,16,512]{2,1,0:T(8,128)(2,1)}) custom-call(bf16[32,16,512]{2,1,0:T(8,128)(2,1)S(1)} %get-tuple-element.6.refs_0_, f32[32,16,512]{2,1,0:T(8,128)S(1)} %get-tuple-element.7.refs_1_, bf16[32,16,512]{2,1,0:T(8,128)(2,1)S(1)} %get-tuple-element.8.refs_2_), custom_call_target="tpu_custom_call" | custom-call | tf_op jit(solution)/shard_map/pallas_call | solution.py:469

commit v6 on v5

--- a/solution.py
+++ b/solution.py
@@ -50,7 +50,7 @@
     cut_refs = [scratch[c * 8:c * 8 + 8] for c in range(NC)]
     own, other, far, from_down, from_up, grad, g_send, g_recv = zip(*cut_refs)
     (
-        table, named_blocks, places,
+        stage, stage_sem, table, named_blocks, places,
         r_send, r_recv, d_send, d_recv, u_send, u_recv,
         first, second, left, right, left_t, total, half, back,
         load_sem, own_sem, pair_send, pair_recv, y_send, y_recv,
@@ -84,7 +84,12 @@
     ]
     owner_load = pltpu.make_async_copy(owners, named_blocks, load_sem.at[5])
     owner_load.start()
+    stages = [
+        pltpu.make_async_copy(grads.at[chips[r], 1 - core, :, :, cols[0]], stage.at[r], stage_sem.at[r])
+        for r in range(NY)
+    ]
     for r in range(NY):
+        stages[r].start()
         owns[0][r].start()
 
     def find_places():
@@ -145,7 +150,7 @@
     pairs = [
         [
             remote(
-                grads.at[chips[r], 1 - core, :, :, cols[c]], other[c].at[r],
+                stage.at[r] if c == 0 else grads.at[chips[r], 1 - core, :, :, cols[c]], other[c].at[r],
                 pair_send.at[c, r], pair_recv.at[c, r], at_pair,
             )
             for r in range(NY)
@@ -154,6 +159,8 @@
     ]
     for c in range(NC):
         for r in range(NY):
+            if c == 0:
+                stages[r].wait()
             pairs[c][r].start()
             if c > 0:
                 owns[c][r].start()
@@ -380,15 +387,6 @@
 
         exchange(u_send, u_recv, (s,), u_ssem.at[s], u_rsem.at[s], fill_plane=undo_left, flat=True)
 
-    for s in range(SLOTS):
-        arrived(u_recv, (s,), u_rsem.at[s], flat=True)
-
-    def pick(j, carry):
-        update[j] = u_recv[places[8, j]]
-        return carry
-
-    lax.fori_loop(0, nb, pick, 0)
-
     for c in range(NC):
         for r in range(NY):
             pairs[c][r].wait_send()
@@ -400,6 +398,15 @@
         arrived(r_send, (s,), r_ssem.at[s])
         arrived(d_send, (s,), d_ssem.at[s])
         arrived(u_send, (s,), u_ssem.at[s])
+
+    for s in range(SLOTS):
+        arrived(u_recv, (s,), u_rsem.at[s], flat=True)
+
+    def pick(j, carry):
+        update[j] = u_recv[places[8, j]]
+        return carry
+
+    lax.fori_loop(0, nb, pick, 0)
 
 
 def deliver(*refs):
@@ -444,6 +451,7 @@
         in_specs=[hbm, hbm, hbm, hbm, hbm, hbm],
         out_specs=(vmem, vmem, vmem),
         scratch_shapes=cut_scratch + [
+            pltpu.VMEM((NY, nb, rows, column_cuts(columns)[1][0]), bf16), dma((NY,)),
             pltpu.VMEM((16, 128), jnp.int32), pltpu.SMEM((nb,), jnp.int32), pltpu.SMEM((16, 128), jnp.int32),
             moved, flat, moved, moved, moved, flat,
             pltpu.VMEM((nb, rows, columns), bf16),

time: 113 us -> 113 us (level)
  no operation moved by 1% of the time
where the time goes in v6:
time: 113 us
  Pallas kernels  112 us (99%)
    pallas_call x1, Pallas kernels, per_device(): pl.pallas_call(functools.partial(kernel, nx, nz), out_shape=(pltpu.VMEM((...  111 us

profile of v6, /device:TPU:8, one launch (start us, length us, event | category | flops | bytes accessed | tf_op | source)
XLA Modules:
  0.0 112.8 jit_solution(7576720860001609812)
XLA Ops:
  0.6 110.8 %shard_map.85 = (bf16[32,16,512]{2,1,0:T(8,128)(2,1)S(1)}, f32[32,16,512]{2,1,0:T(8,128)S(1)}, bf16[32,16,512]{2,1,0:T(8,128)(2,1)S(1)}) custom-call(s32[32]{0:T(128)} %bitcast.7, bf16[4,2,32,16,512]{4,3,2,1,0:T(8,128)(2,1)} %bitcast.4, bf16[32,16,512]{2,1,0:T(8,128)(2,1)} %first_hbm.1, f32[32,16,512]{2,1,0:T(8,128)} %second_hbm.1, ...), custom_call_target="tpu_custom_call" | custom-call | flops 2147483648 | bytes 16777216 | tf_op jit(solution)/shard_map/pallas_call | solution.py:444
  111.4 1.3 %shard_map.86 = (bf16[32,16,512]{2,1,0:T(8,128)(2,1)}, f32[32,16,512]{2,1,0:T(8,128)}, bf16[32,16,512]{2,1,0:T(8,128)(2,1)}) custom-call(bf16[32,16,512]{2,1,0:T(8,128)(2,1)S(1)} %get-tuple-element.6.refs_0_, f32[32,16,512]{2,1,0:T(8,128)S(1)} %get-tuple-element.7.refs_1_, bf16[32,16,512]{2,1,0:T(8,128)(2,1)S(1)} %get-tuple-element.8.refs_2_), custom_call_target="tpu_custom_call" | custom-call | tf_op jit(solution)/shard_map/pallas_call | solution.py:477

commit v7 on v6

--- a/solution.py
+++ b/solution.py
@@ -157,15 +157,9 @@
         ]
         for c in range(NC)
     ]
-    for c in range(NC):
-        for r in range(NY):
-            if c == 0:
-                stages[r].wait()
-            pairs[c][r].start()
-            if c > 0:
-                owns[c][r].start()
-    for load in loads:
-        load.start()
+    for r in range(NY):
+        stages[r].wait()
+        pairs[0][r].start()
 
     low, high = pl.ds(0, nb // 2), pl.ds(nb // 2, nb // 2)
 
@@ -314,6 +308,12 @@
     spread(0)
     for c in range(1, NC):
         if c == 1:
+            for later in range(1, NC):
+                for r in range(NY):
+                    pairs[later][r].start()
+                    owns[later][r].start()
+            for load in loads:
+                load.start()
             hear(1)
             find_places()
             hear(2)

time: 113 us -> 113 us (level)
  no operation moved by 1% of the time
where the time goes in v7:
time: 113 us; the launch traced here: 112 us
  Pallas kernels  112 us (99%)
    pallas_call x1, Pallas kernels, per_device(): pl.pallas_call(functools.partial(kernel, nx, nz), out_shape=(pltpu.VMEM((...  111 us

profile of v7, /device:TPU:8, one launch (start us, length us, event | category | flops | bytes accessed | tf_op | source)
XLA Modules:
  0.0 112.5 jit_solution(7656393196064839837)
XLA Ops:
  0.6 110.5 %shard_map.85 = (bf16[32,16,512]{2,1,0:T(8,128)(2,1)S(1)}, f32[32,16,512]{2,1,0:T(8,128)S(1)}, bf16[32,16,512]{2,1,0:T(8,128)(2,1)S(1)}) custom-call(s32[32]{0:T(128)} %bitcast.7, bf16[4,2,32,16,512]{4,3,2,1,0:T(8,128)(2,1)} %bitcast.4, bf16[32,16,512]{2,1,0:T(8,128)(2,1)} %first_hbm.1, f32[32,16,512]{2,1,0:T(8,128)} %second_hbm.1, ...), custom_call_target="tpu_custom_call" | custom-call | flops 2147483648 | bytes 16777216 | tf_op jit(solution)/shard_map/pallas_call | solution.py:444
  111.1 1.3 %shard_map.86 = (bf16[32,16,512]{2,1,0:T(8,128)(2,1)}, f32[32,16,512]{2,1,0:T(8,128)}, bf16[32,16,512]{2,1,0:T(8,128)(2,1)}) custom-call(bf16[32,16,512]{2,1,0:T(8,128)(2,1)S(1)} %get-tuple-element.6.refs_0_, f32[32,16,512]{2,1,0:T(8,128)S(1)} %get-tuple-element.7.refs_1_, bf16[32,16,512]{2,1,0:T(8,128)(2,1)S(1)} %get-tuple-element.8.refs_2_), custom_call_target="tpu_custom_call" | custom-call | tf_op jit(solution)/shard_map/pallas_call | solution.py:477
